TPU v7x, 256 devices: a whole 4x4x8 slice. The times are simulated.
256 devices in a mesh: ctx: 128 (over y_lo, x, z, core), tp: 2 (over y_hi).
Axes of the slice: x: 4, y: 4 (y_hi: 2, y_lo: 2; y = y_hi * 2 + y_lo), z: 8, core: 2. Of those that a mesh axis runs over, the one named last changes fastest.
Arguments:
- post_gate: bfloat16 [16384, 2048], P('ctx', 'tp'), may hold values from -6 to 6
- pre_gate: bfloat16 [16384, 2048], P('ctx', 'tp'), may hold values from -6 to 6
- features: bfloat16 [16384, 2048], P('ctx', 'tp'), may hold values from -6 to 6
- filters: float32 [16384, 2048], P('ctx', 'tp'), may hold values from -1.1 to 1.1
- token_ids: int32 [16384], P('ctx'), may hold values from 0 to 5
- out_weight: bfloat16 [2048, 2048], P('tp'), may hold values from -0.125 to 0.125
- out_grad: bfloat16 [16384, 2048], P('ctx', 'tp'), may hold values from -6 to 6
Outputs:
- output: bfloat16 [16384, 2048], P('ctx', 'tp')
- grad_post: bfloat16 [16384, 2048], P('ctx', 'tp')
- grad_pre: bfloat16 [16384, 2048], P('ctx', 'tp')
- grad_features: bfloat16 [16384, 2048], P('ctx', 'tp')
All inputs are finite; a program needn't handle non-finite values.
Results may differ from a plain program's by a relative error of at most 0.022.
Values may be sent and summed in bfloat16 or wider, within the bound.
A program may use at most 128 MiB of HBM per device.

v0:
```python
import math

import jax
import jax.numpy as jnp
import numpy as np
from jax import lax
from jax.experimental import pallas as pl
from jax.experimental.pallas import tpu as pltpu
from jax.sharding import PartitionSpec as P

BASES = 4
MESH = pl.DeviceIdType.MESH
F32 = jnp.float32
BF16 = jnp.bfloat16


def tables(n):
    steps = np.arange(n)
    outer = 2 * np.pi * ((2 * steps[:, None] + 1) * steps[None, :] % (4 * n)) / (4 * n)
    twist = 2 * np.pi * ((2 * steps[:, None] + 1) * steps[None, :]) / (4 * n * n)
    inner = 2 * np.pi * (steps[:, None] * steps[None, :] % n) / n
    c, s = np.cos(inner), np.sin(inner)
    as16 = lambda a: jnp.asarray(a.astype(np.float32)).astype(BF16)
    return (
        as16(np.concatenate([np.cos(outer), -np.sin(outer)], 0)),
        as16(np.block([[c, -s], [s, c]])),
        as16(np.block([[c, s], [-s, c]])),
        as16(np.concatenate([np.cos(outer).T, -np.sin(outer).T], 1) / (n * n)),
        jnp.asarray(np.cos(twist).astype(np.float32)),
        jnp.asarray(np.sin(twist).astype(np.float32)),
    )


def dot(a, b):
    return lax.dot_general(a, b, (((1,), (0,)), ((), ())), preferred_element_type=F32)


def dot_nt(a, b):
    return lax.dot_general(a, b, (((1,), (1,)), ((), ())), preferred_element_type=F32)


def kernel(
    post_ref, pre_ref, feat_ref, filt_ref, mask_ref, og_ref, w_hbm,
    f1_ref, m2_ref, m2i_ref, g1_ref, cos_ref, sin_ref,
    out_ref, gpost_ref, gpre_ref, gfeat_ref,
    w_ref, ogo_ref, xh_s, xh_r, g_s, g_r, y_s, y_r, gi_s, gi_r, part_s, part_r, mine_ref,
    grow_ref, gg_ref, wide_ref, back_ref, xs_ref, hs_ref,
    w_sem, s_sem, r_sem,
):
    n = lax.axis_size("ctx")
    me, tp = lax.axis_index("ctx"), lax.axis_index("tp")
    peer = 1 - tp
    tokens, channels = post_ref.shape
    own = channels // n
    cols = pl.ds(pl.multiple_of(tp * channels, channels), channels)
    peer_cols = pl.ds(pl.multiple_of(peer * channels, channels), channels)
    w_copy = pltpu.make_async_copy(w_hbm, w_ref, w_sem)
    w_copy.start()

    barrier = pltpu.get_barrier_semaphore()

    def greet(k, carry):
        pl.semaphore_signal(barrier, inc=1, device_id={"ctx": lax.rem(me + k, n)}, device_id_type=MESH)
        return carry

    lax.fori_loop(1, n, greet, 0)
    pl.semaphore_signal(barrier, inc=1, device_id={"tp": peer}, device_id_type=MESH)

    mask = mask_ref[...]
    per = 128 // own
    for k in range(channels // 128):
        at = slice(128 * k, 128 * k + 128)
        x = pre_ref[:, at].astype(F32) * feat_ref[:, at].astype(F32)
        x = (x.T * mask).reshape(per, own, tokens)
        h = filt_ref[:, at].T.reshape(per, own, tokens)
        xh_s[per * k : per * k + per] = jnp.concatenate([x, h], axis=1).astype(BF16)

    pl.semaphore_wait(barrier, n)

    def to_peer(src, dst, i):
        copy = pltpu.make_async_remote_copy(
            src_ref=src, dst_ref=dst, send_sem=s_sem.at[i], recv_sem=r_sem.at[i],
            device_id={"tp": peer}, device_id_type=MESH,
        )
        copy.start()
        return copy

    def to_all(src, dst, i):
        def go(k, carry):
            to = lax.rem(me + k, n)
            pltpu.make_async_remote_copy(
                src_ref=src.at[to], dst_ref=dst.at[me], send_sem=s_sem.at[i], recv_sem=r_sem.at[i],
                device_id={"ctx": to}, device_id_type=MESH,
            ).start()
            return carry

        lax.fori_loop(1, n, go, 0)
        dst[me] = src[me]
        return pltpu.make_async_remote_copy(
            src_ref=src.at[pl.ds(0, n - 1)], dst_ref=dst.at[pl.ds(0, n - 1)],
            send_sem=s_sem.at[i], recv_sem=r_sem.at[i],
            device_id={"ctx": lax.rem(me + 1, n)}, device_id_type=MESH,
        )

    og_copy = to_peer(og_ref, ogo_ref, 0)
    xh_copy = to_all(xh_s, xh_r, 1)

    w_copy.wait()
    gg_ref[...] = dot_nt(w_ref[:, cols], og_ref[...])
    og_copy.wait_recv()
    gg = gg_ref[...] + dot_nt(w_ref[:, peer_cols], ogo_ref[...])
    gg_ref[...] = gg
    for k in range(channels // 128):
        at = slice(128 * k, 128 * k + 128)
        g = gg_ref[at, :] * post_ref[:, at].astype(F32).T
        g_s[per * k : per * k + per] = g.reshape(per, own, tokens).astype(BF16)
    g_copy = to_all(g_s, g_r, 2)

    cos_t, sin_t = cos_ref[...], sin_ref[...]

    def spectrum(block):
        a = dot(f1_ref[...], block.astype(BF16))
        re, im = a[:n], a[n:]
        b = jnp.concatenate([re * cos_t + im * sin_t, im * cos_t - re * sin_t], axis=1)
        return dot(b.astype(BF16), m2_ref[...])

    def to_signal(re, im):
        d = dot(jnp.concatenate([re, im], axis=1).astype(BF16), m2i_ref[...])
        re, im = d[:, :tokens], d[:, tokens:]
        e = jnp.concatenate([re * cos_t - im * sin_t, im * cos_t + re * sin_t], axis=0)
        return dot(g1_ref[...], e.astype(BF16))

    xh_copy.wait_recv()
    wide_ref[...] = xh_r[...].astype(F32).reshape(n * 2 * own, tokens)
    for c in range(own):
        hs = spectrum(wide_ref[pl.ds(own + c, n, 2 * own), :])
        xs = spectrum(wide_ref[pl.ds(c, n, 2 * own), :])
        hs_ref[c] = hs
        hr, hi, xr, xi = hs[:, :tokens], hs[:, tokens:], xs[:, :tokens], xs[:, tokens:]
        back_ref[pl.ds(c, n, own), :] = to_signal(xr * hr - xi * hi, xr * hi + xi * hr)
    y_s[...] = back_ref[...].reshape(n, own, tokens).astype(BF16)
    y_copy = to_all(y_s, y_r, 3)

    g_copy.wait_recv()
    grow_ref[...] = g_r[...].astype(F32).reshape(n * own, tokens)
    for c in range(own):
        xs = spectrum(grow_ref[pl.ds(c, n, own), :])
        hs = hs_ref[c]
        hr, hi, xr, xi = hs[:, :tokens], hs[:, tokens:], xs[:, :tokens], xs[:, tokens:]
        back_ref[pl.ds(c, n, own), :] = to_signal(xr * hr + xi * hi, xi * hr - xr * hi)
    gi_s[...] = back_ref[...].reshape(n, own, tokens).astype(BF16)
    gi_copy = to_all(gi_s, gi_r, 4)

    y_copy.wait_recv()
    for k in range(channels // 128):
        at = slice(128 * k, 128 * k + 128)
        y = y_r[per * k : per * k + per].astype(F32).reshape(128, tokens)
        xs_ref[:, at] = (post_ref[:, at].astype(F32) * y.T).astype(BF16)
        gpost_ref[:, at] = (gg_ref[at, :] * y).T.astype(BF16)
    part_s[...] = dot(xs_ref[...], w_ref[:, peer_cols]).astype(BF16)
    part_copy = to_peer(part_s, part_r, 5)
    mine_ref[...] = dot(xs_ref[...], w_ref[:, cols])

    gi_copy.wait_recv()
    for k in range(channels // 128):
        at = slice(128 * k, 128 * k + 128)
        gi = gi_r[per * k : per * k + per].astype(F32).reshape(128, tokens)
        gi = (gi * mask).T
        gpre_ref[:, at] = (gi * feat_ref[:, at].astype(F32)).astype(BF16)
        gfeat_ref[:, at] = (gi * pre_ref[:, at].astype(F32)).astype(BF16)

    part_copy.wait_recv()
    out_ref[...] = (mine_ref[...] + part_r[...].astype(F32)).astype(BF16)
    for copy in (og_copy, xh_copy, g_copy, y_copy, gi_copy, part_copy):
        copy.wait_send()


def on_device(post_gate, pre_gate, features, filters, token_ids, out_weight, out_grad):
    tokens, channels = post_gate.shape
    n = lax.axis_size("ctx")
    own = channels // n
    keep = (token_ids < BASES).astype(F32)[None, :]
    vmem = pl.BlockSpec(memory_space=pltpu.VMEM)
    hbm = pl.BlockSpec(memory_space=pl.ANY)
    block = jax.ShapeDtypeStruct((tokens, channels), BF16)
    one = pltpu.VMEM((n, own, tokens), BF16)
    two = pltpu.VMEM((n, 2 * own, tokens), BF16)
    flat = pltpu.VMEM((tokens, channels), BF16)
    return pl.pallas_call(
        kernel,
        out_shape=(block,) * 4,
        in_specs=[vmem] * 6 + [hbm] + [vmem] * 6,
        out_specs=(vmem,) * 4,
        scratch_shapes=[
            pltpu.VMEM(out_weight.shape, BF16), flat, two, two, one, one, one, one, one, one, flat, flat,
            pltpu.VMEM((tokens, channels), F32),
            pltpu.VMEM((n * own, tokens), F32),
            pltpu.VMEM((channels, tokens), F32),
            pltpu.VMEM((n * 2 * own, tokens), F32),
            pltpu.VMEM((n * own, tokens), F32),
            flat,
            pltpu.VMEM((own, n, 2 * tokens), F32),
            pltpu.SemaphoreType.DMA,
            pltpu.SemaphoreType.DMA((6,)),
            pltpu.SemaphoreType.DMA((6,)),
        ],
        compiler_params=pltpu.CompilerParams(
            collective_id=0, has_side_effects=True, vmem_limit_bytes=48 * 2**20
        ),
    )(post_gate, pre_gate, features, filters, keep, out_grad, out_weight, *tables(tokens))


def solution(mesh):
    in_specs = (
        P("ctx", "tp"),
        P("ctx", "tp"),
        P("ctx", "tp"),
        P("ctx", "tp"),
        P("ctx"),
        P("tp", None),
        P("ctx", "tp"),
    )
    out_specs = (P("ctx", "tp"), P("ctx", "tp"), P("ctx", "tp"), P("ctx", "tp"))
    return jax.shard_map(
        on_device, mesh=mesh, in_specs=in_specs, out_specs=out_specs, check_vma=False
    )
```

profile of v0, /device:TPU:1, one launch (start us, length us, event | category | flops | bytes accessed | tf_op | source)
XLA Modules:
  0.0 67.7 jit_solution(10298549352188419215)
XLA Ops:
  0.6 0.7 fusion.mask_ref
  1.3 0.0 copy-start
  1.3 1.0 %copy-done = f32[128,1024]{1,0:T(8,128)S(1)} copy-done((f32[128,1024]{1,0:T(8,128)S(1)}, f32[128,1024]{1,0:T(8,128)}, u32[]{:S(2)}) %copy-start) | copy-done | bytes 524312
  2.3 0.0 copy-start.1
  2.3 0.9 %copy-done.1 = bf16[128,1024]{1,0:T(8,128)(2,1)S(1)} copy-done((bf16[128,1024]{1,0:T(8,128)(2,1)S(1)}, bf16[128,1024]{1,0:T(8,128)(2,1)}, u32[]{:S(2)}) %copy-start.1) | copy-done | bytes 262168
  3.3 0.0 copy-start.2
  3.3 0.9 %copy-done.2 = bf16[128,1024]{1,0:T(8,128)(2,1)S(1)} copy-done((bf16[128,1024]{1,0:T(8,128)(2,1)S(1)}, bf16[128,1024]{1,0:T(8,128)(2,1)}, u32[]{:S(2)}) %copy-start.2) | copy-done | bytes 262168
  4.2 0.0 copy-start.3
  4.2 0.9 %copy-done.3 = bf16[128,1024]{1,0:T(8,128)(2,1)S(1)} copy-done((bf16[128,1024]{1,0:T(8,128)(2,1)S(1)}, bf16[128,1024]{1,0:T(8,128)(2,1)}, u32[]{:S(2)}) %copy-start.3) | copy-done | bytes 262168
  5.2 0.0 copy-start.4
  5.2 0.9 %copy-done.4 = bf16[128,1024]{1,0:T(8,128)(2,1)S(1)} copy-done((bf16[128,1024]{1,0:T(8,128)(2,1)S(1)}, bf16[128,1024]{1,0:T(8,128)(2,1)}, u32[]{:S(2)}) %copy-start.4) | copy-done | bytes 262168
  6.1 0.0 copy-start.5
  6.1 0.9 %copy-done.5 = bf16[256,256]{1,0:T(8,128)(2,1)S(1)} copy-done((bf16[256,256]{1,0:T(8,128)(2,1)S(1)}, bf16[256,256]{1,0:T(8,128)(2,1)}, u32[]{:S(2)}) %copy-start.5) | copy-done | bytes 131096
  7.0 0.0 copy-start.6
  7.0 0.9 %copy-done.6 = bf16[256,256]{1,0:T(8,128)(2,1)S(1)} copy-done((bf16[256,256]{1,0:T(8,128)(2,1)S(1)}, bf16[256,256]{1,0:T(8,128)(2,1)}, u32[]{:S(2)}) %copy-start.6) | copy-done | bytes 131096
  7.9 0.0 copy-start.7
  7.9 0.8 %copy-done.7 = bf16[128,256]{1,0:T(8,128)(2,1)S(1)} copy-done((bf16[128,256]{1,0:T(8,128)(2,1)S(1)}, bf16[128,256]{1,0:T(8,128)(2,1)}, u32[]{:S(2)}) %copy-start.7) | copy-done | bytes 65560
  8.8 0.0 copy-start.8
  8.8 0.8 %copy-done.8 = bf16[256,128]{1,0:T(8,128)(2,1)S(1)} copy-done((bf16[256,128]{1,0:T(8,128)(2,1)S(1)}, bf16[256,128]{1,0:T(8,128)(2,1)}, u32[]{:S(2)}) %copy-start.8) | copy-done | bytes 65560
  9.6 0.0 copy-start.9
  9.6 0.8 %copy-done.9 = f32[128,128]{1,0:T(8,128)S(1)} copy-done((f32[128,128]{1,0:T(8,128)S(1)}, f32[128,128]{1,0:T(8,128)}, u32[]{:S(2)}) %copy-start.9) | copy-done | bytes 65560
  10.5 0.0 copy-start.10
  10.5 0.8 %copy-done.10 = f32[128,128]{1,0:T(8,128)S(1)} copy-done((f32[128,128]{1,0:T(8,128)S(1)}, f32[128,128]{1,0:T(8,128)}, u32[]{:S(2)}) %copy-start.10) | copy-done | bytes 65560
  11.3 53.6 %shard_map.156 = (bf16[128,1024]{1,0:T(8,128)(2,1)S(1)}, bf16[128,1024]{1,0:T(8,128)(2,1)S(1)}, bf16[128,1024]{1,0:T(8,128)(2,1)S(1)}, bf16[128,1024]{1,0:T(8,128)(2,1)S(1)}) custom-call(bf16[128,1024]{1,0:T(8,128)(2,1)S(1)} %copy-done.1, bf16[128,1024]{1,0:T(8,128)(2,1)S(1)} %copy-done.2, bf16[128,1024]{1,0:T(8,128)(2,1)S(1)} %copy-done.3, ...), custom_call_target="tpu_custom_call" | custom-call | tf_op jit(solution)/shard_map/pallas_call | solution.py:189
  64.9 0.7 %copy.21 = bf16[128,1024]{1,0:T(8,128)(2,1)} copy(bf16[128,1024]{1,0:T(8,128)(2,1)S(1)} %get-tuple-element.8) | data formatting | bytes 524288
  65.6 0.7 %copy.22 = bf16[128,1024]{1,0:T(8,128)(2,1)} copy(bf16[128,1024]{1,0:T(8,128)(2,1)S(1)} %get-tuple-element.9) | data formatting | bytes 524288
  66.3 0.7 %copy.23 = bf16[128,1024]{1,0:T(8,128)(2,1)} copy(bf16[128,1024]{1,0:T(8,128)(2,1)S(1)} %get-tuple-element.10) | data formatting | bytes 524288
  67.0 0.7 %copy.24 = bf16[128,1024]{1,0:T(8,128)(2,1)} copy(bf16[128,1024]{1,0:T(8,128)(2,1)S(1)} %get-tuple-element.11) | data formatting | bytes 524288
Async XLA Ops:
  1.3 1.0 %copy-start = (f32[128,1024]{1,0:T(8,128)S(1)}, f32[128,1024]{1,0:T(8,128)}, u32[]{:S(2)}) copy-start(f32[128,1024]{1,0:T(8,128)} %filt_ref.1) | copy-start | bytes 1572868
  2.3 0.9 %copy-start.1 = (bf16[128,1024]{1,0:T(8,128)(2,1)S(1)}, bf16[128,1024]{1,0:T(8,128)(2,1)}, u32[]{:S(2)}) copy-start(bf16[128,1024]{1,0:T(8,128)(2,1)} %post_ref.1) | copy-start | bytes 786436
  3.3 0.9 %copy-start.2 = (bf16[128,1024]{1,0:T(8,128)(2,1)S(1)}, bf16[128,1024]{1,0:T(8,128)(2,1)}, u32[]{:S(2)}) copy-start(bf16[128,1024]{1,0:T(8,128)(2,1)} %pre_ref.1) | copy-start | bytes 786436
  4.2 0.9 %copy-start.3 = (bf16[128,1024]{1,0:T(8,128)(2,1)S(1)}, bf16[128,1024]{1,0:T(8,128)(2,1)}, u32[]{:S(2)}) copy-start(bf16[128,1024]{1,0:T(8,128)(2,1)} %feat_ref.1) | copy-start | bytes 786436
  5.2 0.9 %copy-start.4 = (bf16[128,1024]{1,0:T(8,128)(2,1)S(1)}, bf16[128,1024]{1,0:T(8,128)(2,1)}, u32[]{:S(2)}) copy-start(bf16[128,1024]{1,0:T(8,128)(2,1)} %og_ref.1) | copy-start | bytes 786436
  6.1 0.9 %copy-start.5 = (bf16[256,256]{1,0:T(8,128)(2,1)S(1)}, bf16[256,256]{1,0:T(8,128)(2,1)}, u32[]{:S(2)}) copy-start(bf16[256,256]{1,0:T(8,128)(2,1)} %constant.22.m2i_ref) | copy-start | bytes 393220
  7.0 0.9 %copy-start.6 = (bf16[256,256]{1,0:T(8,128)(2,1)S(1)}, bf16[256,256]{1,0:T(8,128)(2,1)}, u32[]{:S(2)}) copy-start(bf16[256,256]{1,0:T(8,128)(2,1)} %constant.21.m2_ref) | copy-start | bytes 393220
  7.9 0.8 %copy-start.7 = (bf16[128,256]{1,0:T(8,128)(2,1)S(1)}, bf16[128,256]{1,0:T(8,128)(2,1)}, u32[]{:S(2)}) copy-start(bf16[128,256]{1,0:T(8,128)(2,1)} %constant.23.g1_ref) | copy-start | bytes 196612
  8.8 0.8 %copy-start.8 = (bf16[256,128]{1,0:T(8,128)(2,1)S(1)}, bf16[256,128]{1,0:T(8,128)(2,1)}, u32[]{:S(2)}) copy-start(bf16[256,128]{1,0:T(8,128)(2,1)} %constant.20.f1_ref) | copy-start | bytes 196612
  9.6 0.8 %copy-start.9 = (f32[128,128]{1,0:T(8,128)S(1)}, f32[128,128]{1,0:T(8,128)}, u32[]{:S(2)}) copy-start(f32[128,128]{1,0:T(8,128)} %constant.19.clone.sin_ref) | copy-start | bytes 196612
  10.5 0.8 %copy-start.10 = (f32[128,128]{1,0:T(8,128)S(1)}, f32[128,128]{1,0:T(8,128)}, u32[]{:S(2)}) copy-start(f32[128,128]{1,0:T(8,128)} %constant.18.clone.cos_ref) | copy-start | bytes 196612
where the time goes:
time: 68.2 us; the launch traced here: 67.7 us
  Pallas kernels  53.6 us (79%)
  local copies, waits for them, and re-layouts  12.8 us (19%)
    pallas_call x1, Pallas kernels, on_device(): pl.pallas_call(kernel, out_shape=(block,) * 4, in_specs=[vmem] * 6 + [hbm...  53.6 us
    unnamed x26, local copies, waits for them, and re-layouts  12.8 us

commit v1 on v0

v1 whole, which is shorter than its diff:
```python
import math

import jax
import jax.numpy as jnp
import numpy as np
from jax import lax
from jax.experimental import pallas as pl
from jax.experimental.pallas import tpu as pltpu
from jax.sharding import PartitionSpec as P

BASES = 4
MESH = pl.DeviceIdType.MESH
F32 = jnp.float32
BF16 = jnp.bfloat16


def tables(n):
    steps = np.arange(n)
    outer = 2 * np.pi * ((2 * steps[:, None] + 1) * steps[None, :] % (4 * n)) / (4 * n)
    twist = 2 * np.pi * ((2 * steps[:, None] + 1) * steps[None, :]) / (4 * n * n)
    inner = 2 * np.pi * (steps[:, None] * steps[None, :] % n) / n
    c, s = np.cos(inner), np.sin(inner)
    first = np.concatenate([np.cos(outer), -np.sin(outer)], 0)
    coarse = first.astype(jnp.bfloat16).astype(np.float64)
    matrices = [
        np.concatenate([coarse, first - coarse], 1),
        np.block([[c, -s], [s, c]]),
        np.block([[c, s], [-s, c]]),
        np.concatenate([np.cos(outer).T, -np.sin(outer).T], 1) / (n * n),
    ]
    return (
        jnp.asarray(np.concatenate(matrices, 0).astype(np.float32)).astype(BF16),
        jnp.asarray(np.concatenate([np.cos(twist), np.sin(twist)], 0).astype(np.float32)),
    )


def dot(a, b):
    return lax.dot_general(a, b, (((1,), (0,)), ((), ())), preferred_element_type=F32)


def dot_nt(a, b):
    return lax.dot_general(a, b, (((1,), (1,)), ((), ())), preferred_element_type=F32)


def kernel(
    post_hbm, pre_hbm, feat_hbm, filt_hbm, ids_hbm, og_hbm, w_hbm, tab_hbm, twist_hbm,
    out_ref, gpost_ref, gpre_ref, gfeat_ref,
    post_ref, pre_ref, feat_ref, filt_ref, ids_ref, og_ref, w_ref, tab_ref, twist_ref,
    ogo_ref, h_s, h_r, x_s, x_r, g_s, g_r, y_s, y_r, gi_s, gi_r, part_s, part_r, mine_ref,
    gg_ref, flat_ref, rows_ref, mid_ref, hs_ref, xs_ref, e_ref, gated_ref,
    in_sem, s_sem, r_sem,
):
    n = lax.axis_size("ctx")
    me, tp = lax.axis_index("ctx"), lax.axis_index("tp")
    peer = 1 - tp
    tokens, channels = post_ref.shape
    own = channels // n
    loads = {}
    for i, (name, src, dst) in enumerate((
        ("pre", pre_hbm, pre_ref), ("feat", feat_hbm, feat_ref), ("ids", ids_hbm, ids_ref),
        ("filt", filt_hbm, filt_ref), ("og", og_hbm, og_ref), ("w", w_hbm, w_ref),
        ("post", post_hbm, post_ref), ("tab", tab_hbm, tab_ref), ("twist", twist_hbm, twist_ref),
    )):
        loads[name] = pltpu.make_async_copy(src, dst, in_sem.at[i])
        loads[name].start()
    cols = pl.ds(pl.multiple_of(tp * channels, channels), channels)
    peer_cols = pl.ds(pl.multiple_of(peer * channels, channels), channels)

    barrier = pltpu.get_barrier_semaphore()

    def greet(k, carry):
        pl.semaphore_signal(barrier, inc=1, device_id={"ctx": lax.rem(me + k, n)}, device_id_type=MESH)
        return carry

    lax.fori_loop(1, n, greet, 0)
    pl.semaphore_signal(barrier, inc=1, device_id={"tp": peer}, device_id_type=MESH)

    per = 128 // own
    slabs = channels // 128
    loads["filt"].wait()
    for k in range(slabs):
        h = filt_ref[:, 128 * k : 128 * k + 128].T
        h_s[per * k : per * k + per] = h.reshape(per, own, tokens).astype(BF16)

    pl.semaphore_wait(barrier, n)

    def to_peer(src, dst, i):
        copy = pltpu.make_async_remote_copy(
            src_ref=src, dst_ref=dst, send_sem=s_sem.at[i], recv_sem=r_sem.at[i],
            device_id={"tp": peer}, device_id_type=MESH,
        )
        copy.start()
        return copy

    def to_all(src, dst, i):
        def send(dy, dx, dz, dc):
            to = (
                lax.rem(me // 64 + dy, 2) * 64 + lax.rem(me // 16 + dx, 4) * 16
                + lax.rem(me // 2 + dz, 8) * 2 + lax.rem(me + dc, 2)
            )
            pltpu.make_async_remote_copy(
                src_ref=src.at[to], dst_ref=dst.at[me], send_sem=s_sem.at[i], recv_sem=r_sem.at[i],
                device_id={"ctx": to}, device_id_type=MESH,
            ).start()

        for group in ((4,), (3, 5), (2, 6), (1, 7)):
            def ring(p, carry):
                for dz in group:
                    send(lax.rem(p // 2 + 1, 2), lax.rem(6 - p // 4, 4), dz, lax.rem(p, 2))
                return carry

            lax.fori_loop(0, 16, ring, 0)

        def plane(p, carry):
            send(lax.rem(p // 2, 2), p // 4, 0, lax.rem(p, 2))
            return carry

        lax.fori_loop(1, 16, plane, 0)
        dst[me] = src[me]
        return pltpu.make_async_remote_copy(
            src_ref=src.at[pl.ds(0, n - 1)], dst_ref=dst.at[pl.ds(0, n - 1)],
            send_sem=s_sem.at[i], recv_sem=r_sem.at[i],
            device_id={"ctx": lax.rem(me + 1, n)}, device_id_type=MESH,
        )

    loads["og"].wait()
    og_copy = to_peer(og_ref, ogo_ref, 0)
    h_copy = to_all(h_s, h_r, 1)

    for name in ("pre", "feat", "ids"):
        loads[name].wait()
    mask = jnp.where(ids_ref[...] < BASES, 1.0, 0.0)
    for k in range(slabs):
        at = slice(128 * k, 128 * k + 128)
        x = pre_ref[:, at].astype(F32) * feat_ref[:, at].astype(F32)
        x_s[per * k : per * k + per] = (x.T * mask).reshape(per, own, tokens).astype(BF16)
    x_copy = to_all(x_s, x_r, 2)

    for name in ("w", "post", "tab", "twist"):
        loads[name].wait()
    gg_ref[...] = dot_nt(w_ref[:, cols], og_ref[...])
    og_copy.wait_recv()
    gg = gg_ref[...] + dot_nt(w_ref[:, peer_cols], ogo_ref[...])
    gg_ref[...] = gg
    for k in range(slabs):
        at = slice(128 * k, 128 * k + 128)
        g = gg_ref[at, :] * post_ref[:, at].astype(F32).T
        g_s[per * k : per * k + per] = g.reshape(per, own, tokens).astype(BF16)
    g_copy = to_all(g_s, g_r, 3)

    cos_t, sin_t = twist_ref[:n], twist_ref[n:]
    f1_ref, m2_ref, m2i_ref, g1_ref = (
        tab_ref.at[pl.ds(0, 2 * n)], tab_ref.at[pl.ds(2 * n, 2 * n)],
        tab_ref.at[pl.ds(4 * n, 2 * n)], tab_ref.at[pl.ds(6 * n, n)],
    )

    def spectra(received, result):
        flat_ref[...] = received[...].astype(F32).reshape(n * own, tokens)
        for c in range(own):
            block = flat_ref[pl.ds(c, n, own), :].astype(BF16)
            at = slice(tokens * c, tokens * c + tokens)
            rows_ref[:n, at] = block
            rows_ref[n:, at] = block
        for c in range(0, own, 2):
            a = dot(f1_ref[...], rows_ref[:, tokens * c : tokens * (c + 2)])
            for i in range(2):
                re, im = a[:n, tokens * i : tokens * (i + 1)], a[n:, tokens * i : tokens * (i + 1)]
                mid_ref[c + i, :, :tokens] = (re * cos_t + im * sin_t).astype(BF16)
                mid_ref[c + i, :, tokens:] = (im * cos_t - re * sin_t).astype(BF16)
        for c in range(own):
            result[c] = dot(mid_ref[c], m2_ref[...])

    def signals(sign, send):
        for c in range(own):
            hr, hi = hs_ref[c, :, :tokens], hs_ref[c, :, tokens:] * sign
            xr, xi = xs_ref[c, :, :tokens], xs_ref[c, :, tokens:]
            mid_ref[c, :, :tokens] = (xr * hr - xi * hi).astype(BF16)
            mid_ref[c, :, tokens:] = (xr * hi + xi * hr).astype(BF16)
        for c in range(own):
            at = slice(tokens * c, tokens * c + tokens)
            d = dot(mid_ref[c], m2i_ref[...])
            re, im = d[:, :tokens], d[:, tokens:]
            e_ref[:n, at] = (re * cos_t - im * sin_t).astype(BF16)
            e_ref[n:, at] = (im * cos_t + re * sin_t).astype(BF16)
        for c in range(0, own, 2):
            out = dot(g1_ref[...], e_ref[:, tokens * c : tokens * (c + 2)])
            for i in range(2):
                flat_ref[pl.ds(c + i, n, own), :] = out[:, tokens * i : tokens * (i + 1)]
        send[...] = flat_ref[...].reshape(n, own, tokens).astype(BF16)

    h_copy.wait_recv()
    spectra(h_r, hs_ref)
    x_copy.wait_recv()
    spectra(x_r, xs_ref)
    signals(1.0, y_s)
    y_copy = to_all(y_s, y_r, 4)

    g_copy.wait_recv()
    spectra(g_r, xs_ref)
    signals(-1.0, gi_s)
    gi_copy = to_all(gi_s, gi_r, 5)

    y_copy.wait_recv()
    for k in range(slabs):
        at = slice(128 * k, 128 * k + 128)
        y = y_r[per * k : per * k + per].astype(F32).reshape(128, tokens)
        gated_ref[:, at] = (post_ref[:, at].astype(F32) * y.T).astype(BF16)
    part_s[...] = dot(gated_ref[...], w_ref[:, peer_cols]).astype(BF16)
    part_copy = to_peer(part_s, part_r, 6)
    mine_ref[...] = dot(gated_ref[...], w_ref[:, cols])
    for k in range(slabs):
        at = slice(128 * k, 128 * k + 128)
        y = y_r[per * k : per * k + per].astype(F32).reshape(128, tokens)
        gpost_ref[:, at] = (gg_ref[at, :] * y).T.astype(BF16)

    gi_copy.wait_recv()
    for k in range(slabs):
        at = slice(128 * k, 128 * k + 128)
        gi = gi_r[per * k : per * k + per].astype(F32).reshape(128, tokens)
        gi = (gi * mask).T
        gpre_ref[:, at] = (gi * feat_ref[:, at].astype(F32)).astype(BF16)
        gfeat_ref[:, at] = (gi * pre_ref[:, at].astype(F32)).astype(BF16)

    part_copy.wait_recv()
    out_ref[...] = (mine_ref[...] + part_r[...].astype(F32)).astype(BF16)
    for copy in (og_copy, h_copy, x_copy, g_copy, y_copy, gi_copy, part_copy):
        copy.wait_send()


def store(*refs):
    sem = refs[-1]
    copies = [pltpu.make_async_copy(refs[i], refs[4 + i], sem.at[i]) for i in range(4)]
    for copy in copies:
        copy.start()
    for copy in copies:
        copy.wait()


def on_device(post_gate, pre_gate, features, filters, token_ids, out_weight, out_grad):
    tokens, channels = post_gate.shape
    n = lax.axis_size("ctx")
    own = channels // n
    vmem = pl.BlockSpec(memory_space=pltpu.VMEM)
    hbm = pl.BlockSpec(memory_space=pl.ANY)
    block = jax.ShapeDtypeStruct((tokens, channels), BF16)
    one = pltpu.VMEM((n, own, tokens), BF16)
    flat = pltpu.VMEM((tokens, channels), BF16)
    table, twist = tables(tokens)
    results = pl.pallas_call(
        kernel,
        out_shape=(block,) * 4,
        in_specs=[hbm] * 9,
        out_specs=(vmem,) * 4,
        scratch_shapes=[
            flat, flat, flat, pltpu.VMEM((tokens, channels), F32), pltpu.VMEM((1, tokens), jnp.int32), flat,
            pltpu.VMEM(out_weight.shape, BF16), pltpu.VMEM(table.shape, BF16), pltpu.VMEM(twist.shape, F32),
            flat, one, one, one, one, one, one, one, one, one, one, flat, flat,
            pltpu.VMEM((tokens, channels), F32),
            pltpu.VMEM((channels, tokens), F32),
            pltpu.VMEM((n * own, tokens), F32),
            pltpu.VMEM((2 * n, own * tokens), BF16),
            pltpu.VMEM((own, n, 2 * tokens), BF16),
            pltpu.VMEM((own, n, 2 * tokens), F32),
            pltpu.VMEM((own, n, 2 * tokens), F32),
            pltpu.VMEM((2 * n, own * tokens), BF16),
            flat,
            pltpu.SemaphoreType.DMA((9,)),
            pltpu.SemaphoreType.DMA((7,)),
            pltpu.SemaphoreType.DMA((7,)),
        ],
        compiler_params=pltpu.CompilerParams(
            collective_id=0, has_side_effects=True, vmem_limit_bytes=60 * 2**20
        ),
    )(post_gate, pre_gate, features, filters, token_ids.reshape(1, tokens), out_grad, out_weight, table, twist)
    return pl.pallas_call(
        store,
        out_shape=(block,) * 4,
        in_specs=[vmem] * 4,
        out_specs=(hbm,) * 4,
        scratch_shapes=[pltpu.SemaphoreType.DMA((4,))],
    )(*results)


def solution(mesh):
    in_specs = (
        P("ctx", "tp"),
        P("ctx", "tp"),
        P("ctx", "tp"),
        P("ctx", "tp"),
        P("ctx"),
        P("tp", None),
        P("ctx", "tp"),
    )
    out_specs = (P("ctx", "tp"), P("ctx", "tp"), P("ctx", "tp"), P("ctx", "tp"))
    return jax.shard_map(
        on_device, mesh=mesh, in_specs=in_specs, out_specs=out_specs, check_vma=False
    )
```

time: 68.2 us -> 55 us (0.81)
  local copies, waits for them, and re-layouts: 12.8 us -> 0 us
  Pallas kernels: 53.6 us -> 54.3 us
    unnamed x26 -> x0, local copies, waits for them, and re-layouts: 12.8 us -> none
    pallas_call x1 -> x2, Pallas kernels: 53.6 us -> 54.3 us  [the longest x1 52.1 us: on_device(): pl.pallas_call(kernel, out_shape=(block,) * 4, in_specs=[hbm] * 9, out_sp...]
where the time goes in v1:
time: 55 us; the launch traced here: 54.9 us
  Pallas kernels  54.3 us (99%)
  between operations  0.64 us (1%)
    pallas_call x1, Pallas kernels, on_device(): pl.pallas_call(kernel, out_shape=(block,) * 4, in_specs=[hbm] * 9, out_sp...  52.1 us
    pallas_call x1, Pallas kernels, on_device(): pl.pallas_call(store, out_shape=(block,) * 4, in_specs=[vmem] * 4, out_sp...  2.18 us

profile of v1, /device:TPU:1, one launch (start us, length us, event | category | flops | bytes accessed | tf_op | source)
XLA Modules:
  0.0 54.9 jit_solution(9488681995635671139)
XLA Ops:
  0.6 52.1 %shard_map.120 = (bf16[128,1024]{1,0:T(8,128)(2,1)}, bf16[128,1024]{1,0:T(8,128)(2,1)}, bf16[128,1024]{1,0:T(8,128)(2,1)}, bf16[128,1024]{1,0:T(8,128)(2,1)}) custom-call(bf16[128,1024]{1,0:T(8,128)(2,1)} %post_hbm.1, bf16[128,1024]{1,0:T(8,128)(2,1)} %pre_hbm.1, bf16[128,1024]{1,0:T(8,128)(2,1)} %feat_hbm.1, f32[128,1024]{1,0:T(8,128)} %filt_hbm.1, ...), custom_call_target="tpu_custom_call" | custom-call | tf_op jit(solution)/shard_map/pallas_call | solution.py:249
  52.7 2.2 %shard_map.121 = (bf16[128,1024]{1,0:T(8,128)(2,1)}, bf16[128,1024]{1,0:T(8,128)(2,1)}, bf16[128,1024]{1,0:T(8,128)(2,1)}, bf16[128,1024]{1,0:T(8,128)(2,1)}) custom-call(bf16[128,1024]{1,0:T(8,128)(2,1)} %get-tuple-element.8.refs_0_, bf16[128,1024]{1,0:T(8,128)(2,1)} %get-tuple-element.9.refs_1_, bf16[128,1024]{1,0:T(8,128)(2,1)} %get-tuple-element.10.refs_2_, ...), custom_call_target="tpu_custom_call" | custom-call | tf_op jit(solution)/shard_map/pallas_call | solution.py:275

commit v2 on v1

--- a/solution.py
+++ b/solution.py
@@ -48,7 +48,7 @@
     post_ref, pre_ref, feat_ref, filt_ref, ids_ref, og_ref, w_ref, tab_ref, twist_ref,
     ogo_ref, h_s, h_r, x_s, x_r, g_s, g_r, y_s, y_r, gi_s, gi_r, part_s, part_r, mine_ref,
     gg_ref, flat_ref, rows_ref, mid_ref, hs_ref, xs_ref, e_ref, gated_ref,
-    in_sem, s_sem, r_sem,
+    in_sem, s_sem, r_sem, ring_sem,
 ):
     n = lax.axis_size("ctx")
     me, tp = lax.axis_index("ctx"), lax.axis_index("tp")
@@ -57,22 +57,37 @@
     own = channels // n
     loads = {}
     for i, (name, src, dst) in enumerate((
-        ("pre", pre_hbm, pre_ref), ("feat", feat_hbm, feat_ref), ("ids", ids_hbm, ids_ref),
-        ("filt", filt_hbm, filt_ref), ("og", og_hbm, og_ref), ("w", w_hbm, w_ref),
+        ("filt", filt_hbm, filt_ref), ("pre", pre_hbm, pre_ref), ("feat", feat_hbm, feat_ref),
+        ("ids", ids_hbm, ids_ref), ("og", og_hbm, og_ref), ("w", w_hbm, w_ref),
         ("post", post_hbm, post_ref), ("tab", tab_hbm, tab_ref), ("twist", twist_hbm, twist_ref),
     )):
         loads[name] = pltpu.make_async_copy(src, dst, in_sem.at[i])
-        loads[name].start()
+
+    def load(*names):
+        for name in names:
+            loads[name].start()
+
+    load("filt", "pre", "feat", "ids", "og")
     cols = pl.ds(pl.multiple_of(tp * channels, channels), channels)
     peer_cols = pl.ds(pl.multiple_of(peer * channels, channels), channels)
 
+    my_y, my_x, my_z, my_c = me // 64, lax.rem(me // 16, 4), lax.rem(me // 2, 8), lax.rem(me, 2)
+
+    def at_offset(dy, dx, dz, dc):
+        return (
+            lax.rem(my_y + dy, 2) * 64 + lax.rem(my_x + dx, 4) * 16
+            + lax.rem(my_z + dz, 8) * 2 + lax.rem(my_c + dc, 2)
+        )
+
     barrier = pltpu.get_barrier_semaphore()
 
-    def greet(k, carry):
-        pl.semaphore_signal(barrier, inc=1, device_id={"ctx": lax.rem(me + k, n)}, device_id_type=MESH)
-        return carry
-
-    lax.fori_loop(1, n, greet, 0)
+    def greet(semaphore, to):
+        pl.semaphore_signal(semaphore, inc=1, device_id={"ctx": to}, device_id_type=MESH)
+
+    for dz in range(1, 8):
+        greet(barrier, at_offset(0, 0, dz, 0))
+    for p in range(1, 16):
+        greet(barrier, at_offset(p // 2 % 2, p // 4, 0, p % 2))
     pl.semaphore_signal(barrier, inc=1, device_id={"tp": peer}, device_id_type=MESH)
 
     per = 128 // own
@@ -82,7 +97,10 @@
         h = filt_ref[:, 128 * k : 128 * k + 128].T
         h_s[per * k : per * k + per] = h.reshape(per, own, tokens).astype(BF16)
 
-    pl.semaphore_wait(barrier, n)
+    load("w", "post", "tab", "twist")
+    pl.semaphore_wait(barrier, 23)
+    for dz in range(1, 8):
+        greet(ring_sem, at_offset(0, 0, dz, 0))
 
     def to_peer(src, dst, i):
         copy = pltpu.make_async_remote_copy(
@@ -92,12 +110,9 @@
         copy.start()
         return copy
 
-    def to_all(src, dst, i):
-        def send(dy, dx, dz, dc):
-            to = (
-                lax.rem(me // 64 + dy, 2) * 64 + lax.rem(me // 16 + dx, 4) * 16
-                + lax.rem(me // 2 + dz, 8) * 2 + lax.rem(me + dc, 2)
-            )
+    def to_half(src, dst, i, dy):
+        def send(dx, dz, dc):
+            to = at_offset(dy, dx, dz, dc)
             pltpu.make_async_remote_copy(
                 src_ref=src.at[to], dst_ref=dst.at[me], send_sem=s_sem.at[i], recv_sem=r_sem.at[i],
                 device_id={"ctx": to}, device_id_type=MESH,
@@ -106,27 +121,34 @@
         for group in ((4,), (3, 5), (2, 6), (1, 7)):
             def ring(p, carry):
                 for dz in group:
-                    send(lax.rem(p // 2 + 1, 2), lax.rem(6 - p // 4, 4), dz, lax.rem(p, 2))
+                    send(lax.rem(6 - p // 2, 4), dz, lax.rem(p, 2))
                 return carry
 
-            lax.fori_loop(0, 16, ring, 0)
+            lax.fori_loop(0, 8, ring, 0)
 
         def plane(p, carry):
-            send(lax.rem(p // 2, 2), p // 4, 0, lax.rem(p, 2))
+            send(p // 2, 0, lax.rem(p, 2))
             return carry
 
-        lax.fori_loop(1, 16, plane, 0)
-        dst[me] = src[me]
+        lax.fori_loop(1 - dy, 8, plane, 0)
+
+    def all_of(src, dst, i):
         return pltpu.make_async_remote_copy(
             src_ref=src.at[pl.ds(0, n - 1)], dst_ref=dst.at[pl.ds(0, n - 1)],
             send_sem=s_sem.at[i], recv_sem=r_sem.at[i],
             device_id={"ctx": lax.rem(me + 1, n)}, device_id_type=MESH,
         )
 
+    def to_all(src, dst, i):
+        to_half(src, dst, i, 1)
+        to_half(src, dst, i, 0)
+        dst[me] = src[me]
+        return all_of(src, dst, i)
+
     loads["og"].wait()
     og_copy = to_peer(og_ref, ogo_ref, 0)
-    h_copy = to_all(h_s, h_r, 1)
-
+    pl.semaphore_wait(ring_sem, 7)
+    to_half(h_s, h_r, 1, 0)
     for name in ("pre", "feat", "ids"):
         loads[name].wait()
     mask = jnp.where(ids_ref[...] < BASES, 1.0, 0.0)
@@ -134,7 +156,12 @@
         at = slice(128 * k, 128 * k + 128)
         x = pre_ref[:, at].astype(F32) * feat_ref[:, at].astype(F32)
         x_s[per * k : per * k + per] = (x.T * mask).reshape(per, own, tokens).astype(BF16)
-    x_copy = to_all(x_s, x_r, 2)
+    to_half(x_s, x_r, 2, 0)
+    to_half(h_s, h_r, 1, 1)
+    to_half(x_s, x_r, 2, 1)
+    h_r[me] = h_s[me]
+    x_r[me] = x_s[me]
+    h_copy, x_copy = all_of(h_s, h_r, 1), all_of(x_s, x_r, 2)
 
     for name in ("w", "post", "tab", "twist"):
         loads[name].wait()
@@ -205,8 +232,12 @@
         at = slice(128 * k, 128 * k + 128)
         y = y_r[per * k : per * k + per].astype(F32).reshape(128, tokens)
         gated_ref[:, at] = (post_ref[:, at].astype(F32) * y.T).astype(BF16)
-    part_s[...] = dot(gated_ref[...], w_ref[:, peer_cols]).astype(BF16)
-    part_copy = to_peer(part_s, part_r, 6)
+    parts = []
+    half = channels // 2
+    for i in range(2):
+        to = pl.ds(pl.multiple_of(peer * channels + i * half, half), half)
+        part_s[i] = dot(gated_ref[...], w_ref[:, to]).astype(BF16)
+        parts.append(to_peer(part_s.at[i], part_r.at[i], 6 + i))
     mine_ref[...] = dot(gated_ref[...], w_ref[:, cols])
     for k in range(slabs):
         at = slice(128 * k, 128 * k + 128)
@@ -221,9 +252,11 @@
         gpre_ref[:, at] = (gi * feat_ref[:, at].astype(F32)).astype(BF16)
         gfeat_ref[:, at] = (gi * pre_ref[:, at].astype(F32)).astype(BF16)
 
-    part_copy.wait_recv()
-    out_ref[...] = (mine_ref[...] + part_r[...].astype(F32)).astype(BF16)
-    for copy in (og_copy, h_copy, x_copy, g_copy, y_copy, gi_copy, part_copy):
+    for i, copy in enumerate(parts):
+        at = slice(i * half, i * half + half)
+        copy.wait_recv()
+        out_ref[:, at] = (mine_ref[:, at] + part_r[i].astype(F32)).astype(BF16)
+    for copy in (og_copy, h_copy, x_copy, g_copy, y_copy, gi_copy, *parts):
         copy.wait_send()
 
 
@@ -245,16 +278,17 @@
     block = jax.ShapeDtypeStruct((tokens, channels), BF16)
     one = pltpu.VMEM((n, own, tokens), BF16)
     flat = pltpu.VMEM((tokens, channels), BF16)
+    split = pltpu.VMEM((2, tokens, channels // 2), BF16)
     table, twist = tables(tokens)
     results = pl.pallas_call(
         kernel,
-        out_shape=(block,) * 4,
+        out_shape=(pltpu.VMEM((tokens, channels), BF16),) * 4,
         in_specs=[hbm] * 9,
         out_specs=(vmem,) * 4,
         scratch_shapes=[
             flat, flat, flat, pltpu.VMEM((tokens, channels), F32), pltpu.VMEM((1, tokens), jnp.int32), flat,
             pltpu.VMEM(out_weight.shape, BF16), pltpu.VMEM(table.shape, BF16), pltpu.VMEM(twist.shape, F32),
-            flat, one, one, one, one, one, one, one, one, one, one, flat, flat,
+            flat, one, one, one, one, one, one, one, one, one, one, split, split,
             pltpu.VMEM((tokens, channels), F32),
             pltpu.VMEM((channels, tokens), F32),
             pltpu.VMEM((n * own, tokens), F32),
@@ -265,8 +299,9 @@
             pltpu.VMEM((2 * n, own * tokens), BF16),
             flat,
             pltpu.SemaphoreType.DMA((9,)),
-            pltpu.SemaphoreType.DMA((7,)),
-            pltpu.SemaphoreType.DMA((7,)),
+            pltpu.SemaphoreType.DMA((8,)),
+            pltpu.SemaphoreType.DMA((8,)),
+            pltpu.SemaphoreType.REGULAR,
         ],
         compiler_params=pltpu.CompilerParams(
             collective_id=0, has_side_effects=True, vmem_limit_bytes=60 * 2**20
@@ -277,6 +312,7 @@
         out_shape=(block,) * 4,
         in_specs=[vmem] * 4,
         out_specs=(hbm,) * 4,
+        compiler_params=pltpu.CompilerParams(vmem_limit_bytes=8 * 2**20),
         scratch_shapes=[pltpu.SemaphoreType.DMA((4,))],
     )(*results)
 

time: 55 us -> 51.8 us (0.942)
  Pallas kernels: 54.3 us -> 51.1 us
    pallas_call x1, Pallas kernels: 52.1 us -> 50.1 us  [on_device(): pl.pallas_call(kernel, out_shape=(pltpu.VMEM((tokens, channels), BF16),)...]
    pallas_call x1, Pallas kernels: 2.18 us -> 1 us  [on_device(): pl.pallas_call(store, out_shape=(block,) * 4, in_specs=[vmem] * 4, out_sp...]
where the time goes in v2:
time: 51.8 us; the launch traced here: 51.7 us
  Pallas kernels  51.1 us (99%)
  between operations  0.64 us (1%)
    pallas_call x1, Pallas kernels, on_device(): pl.pallas_call(kernel, out_shape=(pltpu.VMEM((tokens, channels), BF16),)...  50.1 us

profile of v2, /device:TPU:1, one launch (start us, length us, event | category | flops | bytes accessed | tf_op | source)
XLA Modules:
  0.0 51.7 jit_solution(611622087154310407)
XLA Ops:
  0.6 50.1 %shard_map.120 = (bf16[128,1024]{1,0:T(8,128)(2,1)S(1)}, bf16[128,1024]{1,0:T(8,128)(2,1)S(1)}, bf16[128,1024]{1,0:T(8,128)(2,1)S(1)}, bf16[128,1024]{1,0:T(8,128)(2,1)S(1)}) custom-call(bf16[128,1024]{1,0:T(8,128)(2,1)} %post_hbm.1, bf16[128,1024]{1,0:T(8,128)(2,1)} %pre_hbm.1, bf16[128,1024]{1,0:T(8,128)(2,1)} %feat_hbm.1, f32[128,1024]{1,0:T(8,128)} %filt_hbm.1, ...), custom_call_target="tpu_custom_call" | custom-call | tf_op jit(solution)/shard_map/pallas_call | solution.py:283
  50.7 1.0 %shard_map.121 = (bf16[128,1024]{1,0:T(8,128)(2,1)}, bf16[128,1024]{1,0:T(8,128)(2,1)}, bf16[128,1024]{1,0:T(8,128)(2,1)}, bf16[128,1024]{1,0:T(8,128)(2,1)}) custom-call(bf16[128,1024]{1,0:T(8,128)(2,1)S(1)} %get-tuple-element.8.refs_0_, bf16[128,1024]{1,0:T(8,128)(2,1)S(1)} %get-tuple-element.9.refs_1_, bf16[128,1024]{1,0:T(8,128)(2,1)S(1)} %get-tuple-element.10.refs_2_, ...), custom_call_target="tpu_custom_call" | custom-call | tf_op jit(solution)/shard_map/pallas_call | solution.py:310

commit v3 on v2

--- a/solution.py
+++ b/solution.py
@@ -46,9 +46,9 @@
     post_hbm, pre_hbm, feat_hbm, filt_hbm, ids_hbm, og_hbm, w_hbm, tab_hbm, twist_hbm,
     out_ref, gpost_ref, gpre_ref, gfeat_ref,
     post_ref, pre_ref, feat_ref, filt_ref, ids_ref, og_ref, w_ref, tab_ref, twist_ref,
-    ogo_ref, h_s, h_r, x_s, x_r, g_s, g_r, y_s, y_r, gi_s, gi_r, part_s, part_r, mine_ref,
+    ogo_ref, h_s, h_r, x_s, x_r, g_s, g_r, y_s, y_r, gi_s, gi_r, gpeer_ref, wp_ref, mine_ref,
     gg_ref, flat_ref, rows_ref, mid_ref, hs_ref, xs_ref, e_ref, gated_ref,
-    in_sem, s_sem, r_sem, ring_sem,
+    in_sem, s_sem, r_sem, ring_sem, ws_sem, wr_sem,
 ):
     n = lax.axis_size("ctx")
     me, tp = lax.axis_index("ctx"), lax.axis_index("tp")
@@ -89,7 +89,13 @@
     for p in range(1, 16):
         greet(barrier, at_offset(p // 2 % 2, p // 4, 0, p % 2))
     pl.semaphore_signal(barrier, inc=1, device_id={"tp": peer}, device_id_type=MESH)
-
+    across = {"ctx": at_offset(1, 0, 0, 0), "tp": peer}
+    pl.semaphore_signal(barrier, inc=1, device_id=across, device_id_type=MESH)
+
+    pl.semaphore_wait(barrier, 24)
+    for dz in range(1, 8):
+        greet(ring_sem, at_offset(0, 0, dz, 0))
+    load("w", "post", "tab", "twist")
     per = 128 // own
     slabs = channels // 128
     loads["filt"].wait()
@@ -97,10 +103,6 @@
         h = filt_ref[:, 128 * k : 128 * k + 128].T
         h_s[per * k : per * k + per] = h.reshape(per, own, tokens).astype(BF16)
 
-    load("w", "post", "tab", "twist")
-    pl.semaphore_wait(barrier, 23)
-    for dz in range(1, 8):
-        greet(ring_sem, at_offset(0, 0, dz, 0))
 
     def to_peer(src, dst, i):
         copy = pltpu.make_async_remote_copy(
@@ -132,18 +134,33 @@
 
         lax.fori_loop(1 - dy, 8, plane, 0)
 
-    def all_of(src, dst, i):
+    def all_of(src, dst, i, count):
         return pltpu.make_async_remote_copy(
-            src_ref=src.at[pl.ds(0, n - 1)], dst_ref=dst.at[pl.ds(0, n - 1)],
+            src_ref=src.at[pl.ds(0, count)], dst_ref=dst.at[pl.ds(0, count)],
             send_sem=s_sem.at[i], recv_sem=r_sem.at[i],
-            device_id={"ctx": lax.rem(me + 1, n)}, device_id_type=MESH,
+            device_id={"ctx": at_offset(0, 0, 0, 1)}, device_id_type=MESH,
         )
 
     def to_all(src, dst, i):
         to_half(src, dst, i, 1)
         to_half(src, dst, i, 0)
         dst[me] = src[me]
-        return all_of(src, dst, i)
+        return all_of(src, dst, i, n - 1)
+
+    def rows_of(x, c, start=0, count=128):
+        return pl.ds(pl.multiple_of((x * 2 + c) * 128 + start, 64), count)
+
+    def pass_weight(src, rows, i, to):
+        copy = pltpu.make_async_remote_copy(
+            src_ref=src, dst_ref=wp_ref.at[rows], send_sem=ws_sem.at[i], recv_sem=wr_sem.at[i],
+            device_id=to, device_id_type=MESH,
+        )
+        copy.start()
+        return copy
+
+    right, left = {"ctx": at_offset(0, 1, 0, 0)}, {"ctx": at_offset(0, 3, 0, 0)}
+    left_x, right_x = lax.rem(my_x + 3, 4), lax.rem(my_x + 1, 4)
+    mine = rows_of(my_x, my_c)
 
     loads["og"].wait()
     og_copy = to_peer(og_ref, ogo_ref, 0)
@@ -161,10 +178,11 @@
     to_half(x_s, x_r, 2, 1)
     h_r[me] = h_s[me]
     x_r[me] = x_s[me]
-    h_copy, x_copy = all_of(h_s, h_r, 1), all_of(x_s, x_r, 2)
+    h_copy, x_copy = all_of(h_s, h_r, 1, n - 1), all_of(x_s, x_r, 2, n - 1)
 
     for name in ("w", "post", "tab", "twist"):
         loads[name].wait()
+    passed = [pass_weight(w_ref.at[mine, peer_cols], mine, 0, across)]
     gg_ref[...] = dot_nt(w_ref[:, cols], og_ref[...])
     og_copy.wait_recv()
     gg = gg_ref[...] + dot_nt(w_ref[:, peer_cols], ogo_ref[...])
@@ -174,6 +192,9 @@
         g = gg_ref[at, :] * post_ref[:, at].astype(F32).T
         g_s[per * k : per * k + per] = g.reshape(per, own, tokens).astype(BF16)
     g_copy = to_all(g_s, g_r, 3)
+    passed[0].wait_recv()
+    passed.append(pass_weight(wp_ref.at[mine], mine, 1, right))
+    passed.append(pass_weight(wp_ref.at[mine], mine, 2, left))
 
     cos_t, sin_t = twist_ref[:n], twist_ref[n:]
     f1_ref, m2_ref, m2i_ref, g1_ref = (
@@ -220,29 +241,51 @@
     x_copy.wait_recv()
     spectra(x_r, xs_ref)
     signals(1.0, y_s)
-    y_copy = to_all(y_s, y_r, 4)
+    to_half(y_s, y_r, 4, 1)
+    to_half(y_s, y_r, 6, 0)
+    y_r[me] = y_s[me]
+    y_copies = all_of(y_s, y_r, 4, n // 2), all_of(y_s, y_r, 6, n // 2 - 1)
+    passed[1].wait_recv()
+    passed[2].wait_recv()
+    rows = rows_of(left_x, my_c, 0, 64)
+    passed.append(pass_weight(wp_ref.at[rows], rows, 3, right))
+    rows = rows_of(right_x, my_c, 64, 64)
+    passed.append(pass_weight(wp_ref.at[rows], rows, 4, left))
 
     g_copy.wait_recv()
     spectra(g_r, xs_ref)
     signals(-1.0, gi_s)
-    gi_copy = to_all(gi_s, gi_r, 5)
-
-    y_copy.wait_recv()
-    for k in range(slabs):
-        at = slice(128 * k, 128 * k + 128)
-        y = y_r[per * k : per * k + per].astype(F32).reshape(128, tokens)
-        gated_ref[:, at] = (post_ref[:, at].astype(F32) * y.T).astype(BF16)
-    parts = []
+    to_half(gi_s, gi_r, 5, 1)
+    gi_r[me] = gi_s[me]
+    gi_copy = all_of(gi_s, gi_r, 5, n - 1)
+
+    passed[3].wait_recv()
+    passed[4].wait_recv()
+    for x in range(4):
+        rows = rows_of(x, my_c)
+        passed.append(pass_weight(wp_ref.at[rows], rows, 5 + x, {"ctx": at_offset(0, 0, 0, 1)}))
+
     half = channels // 2
-    for i in range(2):
-        to = pl.ds(pl.multiple_of(peer * channels + i * half, half), half)
-        part_s[i] = dot(gated_ref[...], w_ref[:, to]).astype(BF16)
-        parts.append(to_peer(part_s.at[i], part_r.at[i], 6 + i))
-    mine_ref[...] = dot(gated_ref[...], w_ref[:, cols])
+    halves = 1 - my_y, my_y
+    gated = []
+    for i, which in enumerate(halves):
+        y_copies[i].wait_recv()
+        for k in range(slabs // 2):
+            at = pl.ds(pl.multiple_of(which * half + 128 * k, 128), 128)
+            y = y_r[pl.ds(which * (n // 2) + per * k, per)].astype(F32).reshape(128, tokens)
+            gated_ref[i, :, 128 * k : 128 * k + 128] = (post_ref[:, at].astype(F32) * y.T).astype(BF16)
+        gated.append(to_peer(gated_ref.at[i], gpeer_ref.at[i], 7 + i))
+        if i == 0:
+            to_half(gi_s, gi_r, 5, 0)
+        rows = pl.ds(pl.multiple_of(which * half, half), half)
+        term = dot(gated_ref[i], w_ref[rows, cols])
+        mine_ref[...] = term if i == 0 else mine_ref[...] + term
     for k in range(slabs):
         at = slice(128 * k, 128 * k + 128)
         y = y_r[per * k : per * k + per].astype(F32).reshape(128, tokens)
         gpost_ref[:, at] = (gg_ref[at, :] * y).T.astype(BF16)
+    for copy in passed[5:]:
+        copy.wait_recv()
 
     gi_copy.wait_recv()
     for k in range(slabs):
@@ -252,11 +295,15 @@
         gpre_ref[:, at] = (gi * feat_ref[:, at].astype(F32)).astype(BF16)
         gfeat_ref[:, at] = (gi * pre_ref[:, at].astype(F32)).astype(BF16)
 
-    for i, copy in enumerate(parts):
-        at = slice(i * half, i * half + half)
-        copy.wait_recv()
-        out_ref[:, at] = (mine_ref[:, at] + part_r[i].astype(F32)).astype(BF16)
-    for copy in (og_copy, h_copy, x_copy, g_copy, y_copy, gi_copy, *parts):
+    for i, which in enumerate(halves):
+        gated[i].wait_recv()
+        rows = pl.ds(pl.multiple_of(which * half, half), half)
+        term = mine_ref[...] + dot(gpeer_ref[i], wp_ref[rows, :])
+        if i == 0:
+            mine_ref[...] = term
+        else:
+            out_ref[...] = term.astype(BF16)
+    for copy in (og_copy, h_copy, x_copy, g_copy, *y_copies, gi_copy, *gated, *passed):
         copy.wait_send()
 
 
@@ -288,7 +335,8 @@
         scratch_shapes=[
             flat, flat, flat, pltpu.VMEM((tokens, channels), F32), pltpu.VMEM((1, tokens), jnp.int32), flat,
             pltpu.VMEM(out_weight.shape, BF16), pltpu.VMEM(table.shape, BF16), pltpu.VMEM(twist.shape, F32),
-            flat, one, one, one, one, one, one, one, one, one, one, split, split,
+            flat, one, one, one, one, one, one, one, one, one, one, split,
+            pltpu.VMEM((channels, channels), BF16),
             pltpu.VMEM((tokens, channels), F32),
             pltpu.VMEM((channels, tokens), F32),
             pltpu.VMEM((n * own, tokens), F32),
@@ -297,11 +345,13 @@
             pltpu.VMEM((own, n, 2 * tokens), F32),
             pltpu.VMEM((own, n, 2 * tokens), F32),
             pltpu.VMEM((2 * n, own * tokens), BF16),
-            flat,
-            pltpu.SemaphoreType.DMA((9,)),
-            pltpu.SemaphoreType.DMA((8,)),
-            pltpu.SemaphoreType.DMA((8,)),
+            split,
+            pltpu.SemaphoreType.DMA((9,)),
+            pltpu.SemaphoreType.DMA((9,)),
+            pltpu.SemaphoreType.DMA((9,)),
             pltpu.SemaphoreType.REGULAR,
+            pltpu.SemaphoreType.DMA((9,)),
+            pltpu.SemaphoreType.DMA((9,)),
         ],
         compiler_params=pltpu.CompilerParams(
             collective_id=0, has_side_effects=True, vmem_limit_bytes=60 * 2**20

time: 51.8 us -> 51 us (0.985)
  Pallas kernels: 51.1 us -> 50.2 us
    pallas_call x1, Pallas kernels: 50.1 us -> 49.2 us  [on_device(): pl.pallas_call(kernel, out_shape=(pltpu.VMEM((tokens, channels), BF16),)...]
where the time goes in v3:
time: 51 us; the launch traced here: 50.9 us
  Pallas kernels  50.2 us (98%)
  between operations  0.64 us (1%)
    pallas_call x1, Pallas kernels, on_device(): pl.pallas_call(kernel, out_shape=(pltpu.VMEM((tokens, channels), BF16),)...  49.2 us

profile of v3, /device:TPU:1, one launch (start us, length us, event | category | flops | bytes accessed | tf_op | source)
XLA Modules:
  0.0 50.9 jit_solution(7425532860549971101)
XLA Ops:
  0.6 49.2 %shard_map.120 = (bf16[128,1024]{1,0:T(8,128)(2,1)S(1)}, bf16[128,1024]{1,0:T(8,128)(2,1)S(1)}, bf16[128,1024]{1,0:T(8,128)(2,1)S(1)}, bf16[128,1024]{1,0:T(8,128)(2,1)S(1)}) custom-call(bf16[128,1024]{1,0:T(8,128)(2,1)} %post_hbm.1, bf16[128,1024]{1,0:T(8,128)(2,1)} %pre_hbm.1, bf16[128,1024]{1,0:T(8,128)(2,1)} %feat_hbm.1, f32[128,1024]{1,0:T(8,128)} %filt_hbm.1, ...), custom_call_target="tpu_custom_call" | custom-call | tf_op jit(solution)/shard_map/pallas_call | solution.py:330
  49.9 1.0 %shard_map.121 = (bf16[128,1024]{1,0:T(8,128)(2,1)}, bf16[128,1024]{1,0:T(8,128)(2,1)}, bf16[128,1024]{1,0:T(8,128)(2,1)}, bf16[128,1024]{1,0:T(8,128)(2,1)}) custom-call(bf16[128,1024]{1,0:T(8,128)(2,1)S(1)} %get-tuple-element.8.refs_0_, bf16[128,1024]{1,0:T(8,128)(2,1)S(1)} %get-tuple-element.9.refs_1_, bf16[128,1024]{1,0:T(8,128)(2,1)S(1)} %get-tuple-element.10.refs_2_, ...), custom_call_target="tpu_custom_call" | custom-call | tf_op jit(solution)/shard_map/pallas_call | solution.py:360

commit v4 on v3

--- a/solution.py
+++ b/solution.py
@@ -98,12 +98,6 @@
     load("w", "post", "tab", "twist")
     per = 128 // own
     slabs = channels // 128
-    loads["filt"].wait()
-    for k in range(slabs):
-        h = filt_ref[:, 128 * k : 128 * k + 128].T
-        h_s[per * k : per * k + per] = h.reshape(per, own, tokens).astype(BF16)
-
-
     def to_peer(src, dst, i):
         copy = pltpu.make_async_remote_copy(
             src_ref=src, dst_ref=dst, send_sem=s_sem.at[i], recv_sem=r_sem.at[i],
@@ -112,6 +106,14 @@
         copy.start()
         return copy
 
+    loads["og"].wait()
+    og_copy = to_peer(og_ref, ogo_ref, 0)
+    loads["filt"].wait()
+    for k in range(slabs):
+        h = filt_ref[:, 128 * k : 128 * k + 128].astype(BF16).T
+        h_s[per * k : per * k + per] = h.reshape(per, own, tokens)
+
+
     def to_half(src, dst, i, dy):
         def send(dx, dz, dc):
             to = at_offset(dy, dx, dz, dc)
@@ -162,8 +164,6 @@
     left_x, right_x = lax.rem(my_x + 3, 4), lax.rem(my_x + 1, 4)
     mine = rows_of(my_x, my_c)
 
-    loads["og"].wait()
-    og_copy = to_peer(og_ref, ogo_ref, 0)
     pl.semaphore_wait(ring_sem, 7)
     to_half(h_s, h_r, 1, 0)
     for name in ("pre", "feat", "ids"):
@@ -172,7 +172,7 @@
     for k in range(slabs):
         at = slice(128 * k, 128 * k + 128)
         x = pre_ref[:, at].astype(F32) * feat_ref[:, at].astype(F32)
-        x_s[per * k : per * k + per] = (x.T * mask).reshape(per, own, tokens).astype(BF16)
+        x_s[per * k : per * k + per] = (x.astype(BF16).T.astype(F32) * mask).reshape(per, own, tokens).astype(BF16)
     to_half(x_s, x_r, 2, 0)
     to_half(h_s, h_r, 1, 1)
     to_half(x_s, x_r, 2, 1)
@@ -189,7 +189,7 @@
     gg_ref[...] = gg
     for k in range(slabs):
         at = slice(128 * k, 128 * k + 128)
-        g = gg_ref[at, :] * post_ref[:, at].astype(F32).T
+        g = gg_ref[at, :] * post_ref[:, at].T.astype(F32)
         g_s[per * k : per * k + per] = g.reshape(per, own, tokens).astype(BF16)
     g_copy = to_all(g_s, g_r, 3)
     passed[0].wait_recv()
@@ -272,8 +272,8 @@
         y_copies[i].wait_recv()
         for k in range(slabs // 2):
             at = pl.ds(pl.multiple_of(which * half + 128 * k, 128), 128)
-            y = y_r[pl.ds(which * (n // 2) + per * k, per)].astype(F32).reshape(128, tokens)
-            gated_ref[i, :, 128 * k : 128 * k + 128] = (post_ref[:, at].astype(F32) * y.T).astype(BF16)
+            y = y_r[pl.ds(which * (n // 2) + per * k, per)].reshape(128, tokens).T
+            gated_ref[i, :, 128 * k : 128 * k + 128] = (post_ref[:, at].astype(F32) * y.astype(F32)).astype(BF16)
         gated.append(to_peer(gated_ref.at[i], gpeer_ref.at[i], 7 + i))
         if i == 0:
             to_half(gi_s, gi_r, 5, 0)
@@ -283,7 +283,7 @@
     for k in range(slabs):
         at = slice(128 * k, 128 * k + 128)
         y = y_r[per * k : per * k + per].astype(F32).reshape(128, tokens)
-        gpost_ref[:, at] = (gg_ref[at, :] * y).T.astype(BF16)
+        gpost_ref[:, at] = (gg_ref[at, :] * y).astype(BF16).T
     for copy in passed[5:]:
         copy.wait_recv()
 
@@ -291,7 +291,7 @@
     for k in range(slabs):
         at = slice(128 * k, 128 * k + 128)
         gi = gi_r[per * k : per * k + per].astype(F32).reshape(128, tokens)
-        gi = (gi * mask).T
+        gi = (gi * mask).astype(BF16).T.astype(F32)
         gpre_ref[:, at] = (gi * feat_ref[:, at].astype(F32)).astype(BF16)
         gfeat_ref[:, at] = (gi * pre_ref[:, at].astype(F32)).astype(BF16)
 

time: 51 us -> 50.7 us (level)
  no operation moved by 1% of the time
where the time goes in v4:
time: 50.7 us; the launch traced here: 50.6 us
  Pallas kernels  50 us (99%)
  between operations  0.64 us (1%)
    pallas_call x1, Pallas kernels, on_device(): pl.pallas_call(kernel, out_shape=(pltpu.VMEM((tokens, channels), BF16),)...  49 us

profile of v4, /device:TPU:1, one launch (start us, length us, event | category | flops | bytes accessed | tf_op | source)
XLA Modules:
  0.0 50.6 jit_solution(18178638890536022079)
XLA Ops:
  0.6 49.0 %shard_map.120 = (bf16[128,1024]{1,0:T(8,128)(2,1)S(1)}, bf16[128,1024]{1,0:T(8,128)(2,1)S(1)}, bf16[128,1024]{1,0:T(8,128)(2,1)S(1)}, bf16[128,1024]{1,0:T(8,128)(2,1)S(1)}) custom-call(bf16[128,1024]{1,0:T(8,128)(2,1)} %post_hbm.1, bf16[128,1024]{1,0:T(8,128)(2,1)} %pre_hbm.1, bf16[128,1024]{1,0:T(8,128)(2,1)} %feat_hbm.1, f32[128,1024]{1,0:T(8,128)} %filt_hbm.1, ...), custom_call_target="tpu_custom_call" | custom-call | tf_op jit(solution)/shard_map/pallas_call | solution.py:330
  49.6 1.0 %shard_map.121 = (bf16[128,1024]{1,0:T(8,128)(2,1)}, bf16[128,1024]{1,0:T(8,128)(2,1)}, bf16[128,1024]{1,0:T(8,128)(2,1)}, bf16[128,1024]{1,0:T(8,128)(2,1)}) custom-call(bf16[128,1024]{1,0:T(8,128)(2,1)S(1)} %get-tuple-element.8.refs_0_, bf16[128,1024]{1,0:T(8,128)(2,1)S(1)} %get-tuple-element.9.refs_1_, bf16[128,1024]{1,0:T(8,128)(2,1)S(1)} %get-tuple-element.10.refs_2_, ...), custom_call_target="tpu_custom_call" | custom-call | tf_op jit(solution)/shard_map/pallas_call | solution.py:360
